TPU v7x, 128 devices: a whole 4x4x4 slice. The times are simulated.
128 devices in a mesh: replica: 8 (over z_lo, y), fsdp: 16 (over z_hi, x, core).
Axes of the slice: x: 4, y: 4, z: 4 (z_hi: 2, z_lo: 2; z = z_hi * 2 + z_lo), core: 2. Of those that a mesh axis runs over, the one named last changes fastest.
Arguments:
- tokens: bfloat16 [65536, 8192], P(('replica', 'fsdp')), may hold values from -6 to 6
- kv_weight: bfloat16 [8, 8192, 1024], P('replica', 'fsdp'), may hold values from -0.0625 to 0.0625
- norm_gain: bfloat16 [8, 8192], P('replica', 'fsdp'), may hold values from 0.099609375 to 1.8984375
- cotangent: bfloat16 [65536, 1024], P(('replica', 'fsdp')), may hold values from -6 to 6
- global_params: float32 [4, 1024, 1024], P(None, 'fsdp'), may hold values from -6 to 6
- momentum: float32 [4, 1024, 1024], P(None, 'fsdp'), may hold values from -3 to 3
- local_params: float32 [8, 1024, 1024], P('replica', 'fsdp'), may hold values from -6 to 6
- fragment_order: int32 [4], replicated, may hold values from 0 to 3, each once
Outputs:
- keys_values: bfloat16 [65536, 1024], P(('replica', 'fsdp'))
- input_grad: bfloat16 [65536, 8192], P(('replica', 'fsdp'))
- weight_grad: float32 [8, 8192, 1024], P('replica', 'fsdp')
- gain_grad: float32 [8, 8192], P('replica', 'fsdp')
- new_params: float32 [4, 1024, 1024], P(None, 'fsdp')
- new_momentum: float32 [4, 1024, 1024], P(None, 'fsdp')
Inputs may be any that keep to these rules, and one draw needn't show every extreme that they name: `fragment_order`: each fragment number appears once; the first entry names the fragment synchronized in this step.
All inputs are finite; a program needn't handle non-finite values.
Results may differ from a plain program's by a relative error of at most 0.025.
Values may be sent and summed in bfloat16 or wider, within the bound.
A program may use at most 192 MiB of HBM per device.

v0:
```python
import jax
import jax.numpy as jnp
from jax import lax
from jax.sharding import PartitionSpec as P

epsilon = 1e-05
outer_beta = 0.9
outer_rate = 0.7


def advance(pieces, scaled, cotangent):
    weight_piece = pieces[0][0]
    gain_piece = pieces[1][0].astype(jnp.float32)
    normed_piece = (scaled * gain_piece).astype(jnp.bfloat16)
    kv_sum = jnp.dot(normed_piece, weight_piece, preferred_element_type=jnp.float32)
    back_piece = jnp.einsum(
        "tc,nc->tn", cotangent, weight_piece, preferred_element_type=jnp.float32
    )
    weighted_piece = gain_piece * back_piece
    row_sums = jnp.sum(weighted_piece * scaled, axis=1)
    gain_part = jnp.sum(back_piece * scaled, axis=0)
    return ((kv_sum, weighted_piece, row_sums, normed_piece, gain_part), normed_piece)


def on_device(
    tokens, kv_weight, norm_gain, cotangent, global_params, momentum, local_params, fragment_order
):
    token_rows, features = tokens.shape
    widened = tokens.astype(jnp.float32)
    inverse_rms = lax.rsqrt(jnp.mean(widened * widened, axis=1, keepdims=True) + epsilon)
    scaled = widened * inverse_rms
    layer_state, normed_piece = advance(
        (
            lax.all_gather(kv_weight, "fsdp", axis=1, tiled=True),
            lax.all_gather(norm_gain, "fsdp", axis=1, tiled=True),
        ),
        scaled,
        cotangent,
    )
    grad_piece = jnp.einsum(
        "tn,tc->nc", normed_piece, cotangent, preferred_element_type=jnp.float32
    )
    grad_rows = grad_piece
    layer_state, grad_rows = (layer_state, grad_rows)
    kv_sum, weighted, row_sums, normed, gain_part = layer_state
    keys_values = kv_sum.astype(jnp.bfloat16)
    input_grad = (inverse_rms * (weighted - scaled * (row_sums[:, None] / features))).astype(
        jnp.bfloat16
    )
    weight_share, gain_share = (
        lax.psum_scatter(
            grad_rows.astype(jnp.bfloat16), "fsdp", scatter_dimension=0, tiled=True
        ).astype(jnp.float32),
        lax.psum_scatter(
            gain_part.astype(jnp.bfloat16), "fsdp", scatter_dimension=0, tiled=True
        ).astype(jnp.float32),
    )
    fragment_slot = fragment_order[0]
    current = lax.dynamic_index_in_dim(global_params, fragment_slot, 0, keepdims=False)
    moment_old = lax.dynamic_index_in_dim(momentum, fragment_slot, 0, keepdims=False)
    drifted = current - local_params[0]
    replicas = lax.axis_size("replica")
    summed = lax.psum(drifted.astype(jnp.bfloat16), "replica").astype(jnp.float32)
    averaged = summed / replicas
    moment = outer_beta * moment_old + averaged
    updated = current - outer_rate * (averaged + outer_beta * moment)
    new_params = lax.dynamic_update_index_in_dim(global_params, updated, fragment_slot, 0)
    new_momentum = lax.dynamic_update_index_in_dim(momentum, moment, fragment_slot, 0)
    return (keys_values, input_grad, weight_share[None], gain_share[None], new_params, new_momentum)


def solution(mesh):
    return jax.shard_map(
        on_device,
        mesh=mesh,
        in_specs=(
            P(("replica", "fsdp"), None),
            P("replica", "fsdp", None),
            P("replica", "fsdp"),
            P(("replica", "fsdp"), None),
            P(None, "fsdp", None),
            P(None, "fsdp", None),
            P("replica", "fsdp", None),
            P(),
        ),
        out_specs=(
            P(("replica", "fsdp"), None),
            P(("replica", "fsdp"), None),
            P("replica", "fsdp", None),
            P("replica", "fsdp"),
            P(None, "fsdp", None),
            P(None, "fsdp", None),
        ),
        check_vma=False,
    )
```

profile of v0, /device:TPU:0, one launch (start us, length us, event | category | flops | bytes accessed | tf_op | source)
XLA Modules:
  0.0 434.6 jit_solution(3294039604773195297)
XLA Ops:
  8.0 0.0 all-reduce.3.cloned.1.call-start
  8.1 1.3 copy.19
  9.4 1.2 copy.20
  12.5 1.6 fusion.22
  14.2 0.0 reduce-scatter.2.cloned.1.call-start
  14.2 25.4 %all_gather.6 = bf16[1,8192]{1,0:T(2,128)(2,1)S(1)} all-gather(bf16[1,512]{1,0:T(2,128)(2,1)} %param.10), channel_id=1, replica_groups=mesh['replica'=8,'fsdp'=16] {'fsdp'}, dimensions={1}, use_global_device_ids=true | all-gather | bytes 17408 | tf_op jit(solution)/shard_map/all_gather | solution.py:35
  39.7 5.1 %fusion.10 = f32[512]{0:T(512)S(1)} fusion(bf16[512,8192]{1,0:T(8,128)(2,1)} %param.8), kind=kLoop, calls=%fused_computation.12 | loop fusion | flops 12582400 | bytes 8390656 | tf_op jit(solution)/shard_map/reduce_sum | solution.py:30
  44.8 16.4 %convolution_convert_fusion = bf16[8192,1024]{1,0:T(8,128)(2,1)} fusion(bf16[512,1024]{1,0:T(8,128)(2,1)S(1)} %copy-done, bf16[512,8192]{1,0:T(8,128)(2,1)} %param.8, f32[8192]{0:T(1024)S(1)} %bitcast.36, f32[512]{0:T(512)S(1)} %add_rsqrt_fusion), kind=kOutput, calls=%fused_computation.17 | convolution fusion | flops 8615100416 | bytes 26249216 | tf_op jit(solution)/shard_map/tn,tc->nc/dot_general | solution.py:40
  61.3 0.0 reduce-scatter.2.cloned.1.call-update
  61.3 0.2 all-gather.2.cloned.1.call-start
  61.5 0.4 all-gather.2.cloned.1.call-update
  61.9 0.0 copy-done.4
  61.9 0.6 dynamic-slice
  63.2 27.0 %all-reduce.3.cloned.1.call-done = bf16[64,1024]{1,0:T(8,128)(2,1)} async-done(((bf16[64,1024]{1,0:T(8,128)(2,1)}), bf16[64,1024]{1,0:T(8,128)(2,1)}) %all-reduce.3.cloned.1.call-update) | async-done | bytes 131088 | tf_op jit(solution)/shard_map/psum | solution.py:63
  90.2 0.9 bitcast_add_fusion
  91.2 1.0 bitcast_dynamic-update-slice_fusion
  92.2 112.3 %reduce-scatter.2.cloned.1.call-done = bf16[512,1024]{1,0:T(8,128)(2,1)} async-done(((bf16[8192,1024]{1,0:T(8,128)(2,1)}), bf16[512,1024]{1,0:T(8,128)(2,1)}) %reduce-scatter.2.cloned.1.call-update) | async-done | bytes 1048592 | tf_op jit(solution)/shard_map/reduce_scatter | solution.py:51
  204.5 2.8 bitcast_convert_fusion
  207.3 107.4 %all-gather.2.cloned.1.call-done = bf16[1,8192,1024]{2,1,0:T(8,128)(2,1)} async-done(((bf16[1,512,1024]{2,1,0:T(8,128)(2,1)}), bf16[1,8192,1024]{2,1,0:T(8,128)(2,1)}) %all-gather.2.cloned.1.call-update) | async-done | bytes 16777232 | tf_op jit(solution)/shard_map/all_gather | solution.py:34
  314.7 18.3 %fusion.9 = (bf16[8192]{0:T(1024)(128)(2,1)S(1)}, f32[512]{0:T(512)S(1)}, f32[512,8192]{1,0:T(8,128)}) fusion(bf16[512,8192]{1,0:T(8,128)(2,1)} %param.8, f32[512]{0:T(512)S(1)} %add_rsqrt_fusion, f32[8192]{0:T(1024)S(1)} %bitcast.37, bf16[512,1024]{1,0:T(8,128)(2,1)S(1)} %copy-done, bf16[1,8192,1024]{2,1,0:T(8,128)(2,1)} %all-gather.2.cloned.1.call-done), kind=kOutput, calls=%fused_computation.11 | convolution fusion | flops 8619286528 | bytes 43044864 | tf_op jit(solution)/shard_map/tc,nc->tn/dot_general | solution.py:16
  333.1 65.3 %all-reduce = bf16[8192]{0:T(1024)(128)(2,1)S(1)} all-reduce(bf16[8192]{0:T(1024)(128)(2,1)S(1)} %get-tuple-element.6), channel_id=3, replica_groups=mesh['replica'=8,'fsdp'=16] {'fsdp'}, use_global_device_ids=true, to_apply=%region_4.0.clone | all-reduce | flops 8192 | bytes 32768
  398.4 12.4 %fusion.8 = bf16[512,8192]{1,0:T(8,128)(2,1)} fusion(bf16[512,8192]{1,0:T(8,128)(2,1)} %param.8, f32[512,8192]{1,0:T(8,128)} %get-tuple-element.10, f32[512]{0:T(512)S(1)} %broadcast_multiply_fusion, f32[8192]{0:T(1024)S(1)} %bitcast.38, f32[512]{0:T(512)S(1)} %add_rsqrt_fusion), kind=kLoop, calls=%fused_computation.10 | loop fusion | flops 29360128 | bytes 33591296 | tf_op jit(solution)/shard_map/convert_element_type | solution.py:47
  410.8 0.7 dynamic-slice_convert_fusion
  411.5 15.7 %fusion.17 = bf16[512,1024]{1,0:T(8,128)(2,1)} fusion(bf16[1,8192,1024]{2,1,0:T(8,128)(2,1)} %all-gather.2.cloned.1.call-done, bf16[512,8192]{1,0:T(8,128)(2,1)} %param.8, f32[8192]{0:T(1024)S(1)} %bitcast.39, f32[512]{0:T(512)S(1)} %add_rsqrt_fusion), kind=kOutput, calls=%fused_computation.18 | convolution fusion | flops 8607236096 | bytes 26249216 | tf_op jit(solution)/shard_map/dot_general | solution.py:15
  (14 shorter events, 0.1 us)
Async XLA Ops:
  8.0 36.8 %copy-start = (bf16[512,1024]{1,0:T(8,128)(2,1)S(1)}, bf16[512,1024]{1,0:T(8,128)(2,1)}, u32[]{:S(2)}) copy-start(bf16[512,1024]{1,0:T(8,128)(2,1)} %param.11) | copy-start | bytes 3145732
  8.0 82.2 %all-reduce.3.cloned.1.call-start = ((), (), s32[]{:S(2)}) async-start(), calls=%async_computation.3 | async-start | bytes 262144 | tf_op jit(solution)/shard_map/psum | solution.py:63
  14.2 190.3 %reduce-scatter.2.cloned.1.call-start = ((), (), s32[]{:S(2)}) async-start(), calls=%async_computation.2 | async-start | bytes 17825792 | tf_op jit(solution)/shard_map/reduce_scatter | solution.py:51
  61.3 0.7 copy-start.4
  61.3 253.4 %all-gather.2.cloned.1.call-start = ((), (), s32[]{:S(2)}) async-start(), calls=%async_computation.1 | async-start | bytes 17825792 | tf_op jit(solution)/shard_map/all_gather | solution.py:34
  92.2 240.9 %copy-start.2 = (f32[4,64,1024]{2,1,0:T(8,128)}, f32[4,64,1024]{2,1,0:T(8,128)S(1)}, u32[]{:S(2)}) copy-start(f32[4,64,1024]{2,1,0:T(8,128)S(1)} %get-tuple-element.9) | copy-start | bytes 3145732
  92.2 240.9 %copy-start.3 = (f32[4,64,1024]{2,1,0:T(8,128)}, f32[4,64,1024]{2,1,0:T(8,128)S(1)}, u32[]{:S(2)}) copy-start(f32[4,64,1024]{2,1,0:T(8,128)S(1)} %get-tuple-element.8) | copy-start | bytes 3145732
  411.5 15.7 %copy-start.1 = (bf16[512,1024]{1,0:T(8,128)(2,1)S(1)}, bf16[512,1024]{1,0:T(8,128)(2,1)}, u32[]{:S(2)}) copy-start(bf16[512,1024]{1,0:T(8,128)(2,1)} %param.11) | copy-start | bytes 3145732
Sparse Core Ops, SparseCore 0:
  14.3 75.8 all-reduce.2
Sparse Core Ops, SparseCore 1:
  61.4 143.1 reduce-scatter.1
  207.2 107.5 all-gather.1
where the time goes:
time: 435 us
  waiting for transfers between devices  247 us (57%)
  blocking collectives  90.7 us (21%)
  matrix products  50.5 us (12%)
  other arithmetic  24.6 us (6%)
  between operations  18.2 us (4%)
    reduce_scatter x1, waiting for transfers between devices, on_device(): lax.psum_scatter(grad_rows.astype(jnp.bfloat16), 'fsdp', scatter_dimensio...  112 us
    all_gather x1, waiting for transfers between devices, on_device(): lax.all_gather(kv_weight, 'fsdp', axis=1, tiled=True)  107 us
    unnamed x1, blocking collectives  65.3 us
    psum x1, waiting for transfers between devices, on_device(): lax.psum(drifted.astype(jnp.bfloat16), 'replica').astype(jnp.float32)  27 us
    all_gather x1, blocking collectives, on_device(): lax.all_gather(norm_gain, 'fsdp', axis=1, tiled=True)  25.4 us
    dot_general x1, matrix products, advance(): jnp.einsum('tc,nc->tn', cotangent, weight_piece, preferred_element_type=j...  18.3 us
    dot_general x1, matrix products, on_device(): jnp.einsum('tn,tc->nc', normed_piece, cotangent, preferred_element_type=j...  16.4 us
    dot_general x1, matrix products, advance(): jnp.dot(normed_piece, weight_piece, preferred_element_type=jnp.float32)  15.7 us
  transfers between devices with their start and end apart: 3, of which 3 were waited for; matrix products, arithmetic and copies ran while one was open for 6% of the time, Pallas kernels for 0%

commit v1 on v0

v1 whole, which is shorter than its diff:
```python
import functools

import jax
import jax.numpy as jnp
from jax import lax
from jax.experimental import pallas as pl
from jax.experimental.pallas import tpu as pltpu
from jax.sharding import PartitionSpec as P

epsilon = 1e-05
outer_beta = 0.9
outer_rate = 0.7
f32 = jnp.float32
bf16 = jnp.bfloat16
MESH = pl.DeviceIdType.MESH
LANES = 128


def split_rows(rows):
    first = max(32, rows * 9 // 16 // 32 * 32)
    return first, rows - first, first // 2, (rows - first) // 2


def layer_kernel(
    features, tok_hbm, gw_hbm, cot_hbm, kv_out, ig_out, u_out,
    tok, w, u, cot, cots, kvp, kvx, sq, sq_in, inv, rs, rs_in,
    ra_opp, rb_z, rb_opp, ra_x, rb_x, ra_z, send_sem, recv_sem, local_sem,
):
    rows, cols = gw_hbm.shape
    toks = tok_hbm.shape[0]
    RA, RB, HA, HB = split_rows(rows)
    r = lax.axis_index("replica")
    me = lax.axis_index("fsdp")
    zh = lax.div(me, 8)
    x = lax.rem(lax.div(me, 2), 4)
    c = lax.rem(me, 2)

    def at(plane, col, core):
        return (r, plane * 8 + col * 2 + core)

    right = at(zh, lax.rem(x + 1, 4), c)
    left = at(zh, lax.rem(x + 3, 4), c)
    partner = at(1 - zh, x, c)
    sibling = at(zh, x, 1 - c)

    def slot(plane, dx):
        return (zh if plane == 0 else 1 - zh) * 4 + lax.rem(x + dx + 4, 4)

    barrier = pltpu.get_barrier_semaphore()
    for other in (right, left, partner, sibling):
        pl.semaphore_signal(barrier, inc=1, device_id=other, device_id_type=MESH)
    pl.semaphore_wait(barrier, 4)

    sent = {}

    def send(name, src, dst, to):
        i = len(sent)
        copy = pltpu.make_async_remote_copy(
            src_ref=src, dst_ref=dst, send_sem=send_sem.at[i], recv_sem=recv_sem.at[i],
            device_id=to, device_id_type=MESH,
        )
        copy.start()
        sent[name] = copy

    def got(*names):
        for name in names:
            sent[name].wait_recv()

    a_rows, b_rows = pl.ds(0, RA), pl.ds(RA, RB)
    a_first, a_last = pl.ds(0, HA), pl.ds(HA, RA - HA)
    b_first, b_last = pl.ds(RA, HB), pl.ds(RA + HB, RB - HB)

    own = slot(0, 0)
    send("g_right_b", gw_hbm.at[b_rows], w.at[own, b_rows], right)
    send("g_left_b", gw_hbm.at[b_rows], w.at[own, b_rows], left)
    send("g_z_a", gw_hbm.at[a_rows], w.at[own, a_rows], partner)
    send("g_right_a", gw_hbm.at[a_rows], w.at[own, a_rows], right)
    send("g_left_a", gw_hbm.at[a_rows], w.at[own, a_rows], left)
    send("g_z_b", gw_hbm.at[b_rows], w.at[own, b_rows], partner)

    def columns(k, core):
        return pl.ds(pl.multiple_of((2 * k + core) * rows, rows), rows)

    blocks = features // rows // 2
    loads = []
    for k in range(blocks):
        load = pltpu.make_async_copy(tok_hbm.at[:, columns(k, c)], tok.at[0, k], local_sem.at[k])
        load.start()
        loads.append(load)
        send(f"t{k}", tok_hbm.at[:, columns(k, 1 - c)], tok.at[1, k], sibling)
    load_cot = pltpu.make_async_copy(cot_hbm, cot.at[0], local_sem.at[blocks])
    load_cot.start()
    send("cot", cot_hbm, cot.at[1], sibling)
    load_w = pltpu.make_async_copy(gw_hbm, w.at[own], local_sem.at[blocks + 1])
    load_w.start()

    RT = min(64, toks)
    lanes = min(LANES, rows)

    def square_block(half, k, fresh):
        @pl.loop(0, toks // RT)
        def _(i):
            at_rows = pl.ds(pl.multiple_of(i * RT, RT), RT)
            piece = tok[half, k, at_rows, :].astype(f32)
            piece = piece * piece
            total = piece[:, :lanes]
            for j in range(1, rows // lanes):
                total = total + piece[:, j * lanes : (j + 1) * lanes]
            if fresh:
                sq[half, at_rows, :] = total
            else:
                sq[half, at_rows, :] += total

    for half in range(2):
        for k in range(blocks):
            if half == 0:
                loads[k].wait()
            else:
                got(f"t{k}")
            square_block(half, k, k == 0)
    send("sq", sq, sq_in, sibling)
    load_cot.wait()
    got("cot", "sq")

    def wide(column, width):
        return jnp.concatenate([column] * (width // lanes), axis=1) if width > lanes else column[:, :width]

    for half in range(2):
        @pl.loop(0, toks // RT)
        def _(i):
            at_rows = pl.ds(pl.multiple_of(i * RT, RT), RT)
            total = sq[half, at_rows, :] + sq_in[1 - half, at_rows, :]
            mean = jnp.sum(total, axis=1, keepdims=True) / features
            root = jnp.broadcast_to(lax.rsqrt(mean + epsilon), (RT, lanes))
            inv[half, at_rows, :] = root
            cots[half, at_rows, :] = (cot[half, at_rows, :].astype(f32) * wide(root, cols)).astype(bf16)

    FT = min(256, rows)
    TT = min(256, toks)

    def u_block(k):
        @pl.loop(0, rows // FT)
        def _(j):
            at_rows = pl.ds(pl.multiple_of(j * FT, FT), FT)
            total = None
            for half in range(2):
                term = lax.dot_general(
                    tok[half, k, :, at_rows], cots[half], (((0,), (0,)), ((), ())),
                    preferred_element_type=f32,
                )
                total = term if total is None else total + term
            u[k, at_rows, :] = total.astype(bf16)

    def kv_block(k, fresh=False):
        for half in range(2):
            @pl.loop(0, toks // TT)
            def _(j):
                at_rows = pl.ds(pl.multiple_of(j * TT, TT), TT)
                term = jnp.dot(tok[half, k, at_rows, :], w[k], preferred_element_type=f32)
                if fresh:
                    kvp[half, at_rows, :] = term
                else:
                    kvp[half, at_rows, :] += term

    def back_block(k):
        for half in range(2):
            @pl.loop(0, toks // TT)
            def _(j):
                at_rows = pl.ds(pl.multiple_of(j * TT, TT), TT)
                weighted = lax.dot_general(
                    cot[half, at_rows, :], w[k], (((1,), (1,)), ((), ())),
                    preferred_element_type=f32,
                )
                grad = weighted * wide(inv[half, at_rows, :], rows) - tok[
                    half, k, at_rows, :
                ].astype(f32) * wide(sq[half, at_rows, :], rows)
                tok[half, k, at_rows, :] = grad.astype(bf16)

    ig_base = 64

    def ig_store(k):
        return pltpu.make_async_copy(
            tok.at[0, k], ig_out.at[:, columns(k, c)], local_sem.at[blocks + 2 + k]
        )

    def ig_send(k):
        return pltpu.make_async_remote_copy(
            src_ref=tok.at[1, k], dst_ref=ig_out.at[:, columns(k, c)],
            send_sem=send_sem.at[ig_base + k], recv_sem=recv_sem.at[ig_base + k],
            device_id=sibling, device_id_type=MESH,
        )

    def back_loop(lo, hi):
        @pl.loop(lo, hi)
        def _(k):
            back_block(k)
            ig_store(k).start()
            ig_send(k).start()

    AT = 16

    def add_rows(count, dst, dst_at, *srcs):
        @pl.loop(0, count // AT)
        def _(i):
            to = pl.ds(pl.multiple_of(dst_at + i * AT, AT), AT)
            total = u[dst, to, :].astype(f32)
            for ref, index in srcs:
                total = total + ref[(*index, pl.ds(pl.multiple_of(i * AT, AT), AT), slice(None))].astype(f32)
            u[dst, to, :] = total.astype(bf16)

    def reduce_a(plane):
        got(f"ro_r{plane}", f"ro_l{plane}")
        to_right, to_left = slot(plane, 1), slot(plane, -1)
        add_rows(HA, to_right, 0, (ra_opp, (0, plane)))
        send(f"ra_r{plane}", u.at[to_right, a_rows], ra_x.at[0, plane], right)
        add_rows(RA - HA, to_left, HA, (ra_opp, (1, plane)))
        send(f"ra_l{plane}", u.at[to_left, a_rows], ra_x.at[1, plane], left)

    def reduce_b_opposite():
        got("rz0")
        add_rows(RB, mine_o, RA, (rb_z, (0,)))
        send("rbo_r", u.at[mine_o, b_first], rb_opp.at[0, pl.ds(0, HB)], right)
        send("rbo_l", u.at[mine_o, b_last], rb_opp.at[1, pl.ds(0, RB - HB)], left)
        got("rz1")
        add_rows(RB, mine_r, RA, (rb_z, (1,)))
        got("rz2")
        add_rows(RB, mine_l, RA, (rb_z, (2,)))

    def reduce_b_side():
        got("rbo_r", "rbo_l")
        add_rows(HB, mine_r, RA, (rb_opp, (0,)))
        send("rb_r", u.at[mine_r, b_rows], rb_x.at[0], right)
        add_rows(RB - HB, mine_l, RA + HB, (rb_opp, (1,)))
        send("rb_l", u.at[mine_l, b_rows], rb_x.at[1], left)

    def u_loop(lo, hi):
        @pl.loop(lo, hi)
        def _(k):
            u_block(k)

    mine_r, mine_l, mine_o = slot(0, 1), slot(0, -1), slot(0, 2)
    far, far_r, far_l, far_o = slot(1, 0), slot(1, 1), slot(1, -1), slot(1, 2)
    got("g_right_b", "g_left_b", "g_z_a")
    send("g2_right_b", w.at[mine_l, b_first], w.at[mine_l, b_first], right)
    send("g2_left_b", w.at[mine_r, b_last], w.at[mine_r, b_last], left)
    send("gz_l", w.at[mine_l, b_rows], w.at[mine_l, b_rows], partner)
    send("gz_r", w.at[mine_r, b_rows], w.at[mine_r, b_rows], partner)
    send("h_right_a", w.at[far, a_rows], w.at[far, a_rows], right)
    send("h_left_a", w.at[far, a_rows], w.at[far, a_rows], left)
    u_loop(0, 3)
    got("g_right_a", "g_left_a")
    send("g2_right_a", w.at[mine_l, a_first], w.at[mine_l, a_first], right)
    send("g2_left_a", w.at[mine_r, a_last], w.at[mine_r, a_last], left)
    u_loop(3, 6)
    got("g2_right_b", "g2_left_b")
    send("gz_o", w.at[mine_o, b_rows], w.at[mine_o, b_rows], partner)
    u_loop(6, 8)
    for j, dx in enumerate((2, 1, -1, 0)):
        send(f"rz{j}", u.at[slot(1, dx), b_rows], rb_z.at[j], partner)
    load_w.wait()
    kv_block(own, True)

    @pl.loop(0, 2)
    def _(i):
        kv_block(zh * 4 + lax.rem(x + 1 + 2 * i, 4))

    got("h_right_a", "h_left_a")
    send("h2_right_a", w.at[far_l, a_first], w.at[far_l, a_first], right)
    send("h2_left_a", w.at[far_r, a_last], w.at[far_r, a_last], left)
    for plane in (1, 0):
        opp = slot(plane, 2)
        send(f"ro_r{plane}", u.at[opp, a_first], ra_opp.at[0, plane, pl.ds(0, HA)], right)
        send(f"ro_l{plane}", u.at[opp, a_last], ra_opp.at[1, plane, pl.ds(0, RA - HA)], left)
    got("g2_right_a", "g2_left_a", "g_z_b")
    kv_block(mine_o)
    kv_block(far)
    got("gz_l", "gz_r", "h2_right_a", "h2_left_a", "gz_o")

    @pl.loop(1, 4)
    def _(i):
        kv_block((1 - zh) * 4 + lax.rem(x + i, 4))

    send("kv", kvp.at[1], kvx, sibling)
    for half in range(2):
        @pl.loop(0, toks // RT)
        def _(i):
            at_rows = pl.ds(pl.multiple_of(i * RT, RT), RT)
            piece = kvp[half, at_rows, :] * cot[half, at_rows, :].astype(f32)
            total = piece[:, :lanes]
            for j in range(1, cols // lanes):
                total = total + piece[:, j * lanes : (j + 1) * lanes]
            rs[half, at_rows, :] = total

    send("rs", rs, rs_in, sibling)
    reduce_a(1)
    sent["sq"].wait_send()
    got("rs", "kv")
    for half in range(2):
        @pl.loop(0, toks // RT)
        def _(i):
            at_rows = pl.ds(pl.multiple_of(i * RT, RT), RT)
            scale = inv[half, at_rows, :]
            total = jnp.sum(rs[half, at_rows, :] + rs_in[1 - half, at_rows, :], axis=1, keepdims=True)
            sq[half, at_rows, :] = (jnp.broadcast_to(total, (RT, lanes)) * scale / features) * scale * scale
            if half == 0:
                whole = kvp[0, at_rows, :] + kvx[at_rows, :]
                cots[0, at_rows, :] = (whole * wide(scale, cols)).astype(bf16)

    store_kv = pltpu.make_async_copy(cots.at[0], kv_out, local_sem.at[2 * blocks + 2])
    store_kv.start()

    back_loop(0, 2)
    reduce_b_opposite()
    reduce_a(0)
    back_loop(2, 5)
    reduce_b_side()
    back_loop(5, 8)
    got("ra_r1", "ra_l1")
    add_rows(RA, far, 0, (ra_x, (0, 1)), (ra_x, (1, 1)))
    send("za", u.at[far, a_rows], ra_z, partner)
    got("rz3")
    add_rows(RB, own, RA, (rb_z, (3,)))

    store_kv.wait()

    def last_sum(lo, count, *srcs):
        @pl.loop(0, count // AT)
        def _(i):
            to = pl.ds(pl.multiple_of(lo + i * AT, AT), AT)
            total = u[own, to, :].astype(f32)
            for ref, index in srcs:
                total = total + ref[(*index, pl.ds(pl.multiple_of(i * AT, AT), AT), slice(None))].astype(f32)
            kvx[to, :] = total
        store = pltpu.make_async_copy(
            kvx.at[pl.ds(lo, count)], u_out.at[pl.ds(lo, count)], local_sem.at[2 * blocks + 3 + (lo > 0)]
        )
        store.start()
        return store

    got("rb_r", "rb_l")
    last_b = last_sum(RA, RB, (rb_x, (0,)), (rb_x, (1,)))
    got("ra_r0", "ra_l0", "za")
    last_a = last_sum(0, RA, (ra_x, (0, 0)), (ra_x, (1, 0)), (ra_z, ()))
    for name, copy in sent.items():
        if name != "sq":
            copy.wait_send()

    @pl.loop(0, blocks)
    def _(k):
        ig_store(k).wait()
        ig_send(k).wait()

    last_b.wait()
    last_a.wait()


def layer(tokens, gained, cotangent):
    toks, features = tokens.shape
    rows, cols = gained.shape
    blocks = features // rows // 2
    RA, RB, HA, HB = split_rows(rows)
    lanes = min(LANES, rows)
    any_space = pl.BlockSpec(memory_space=pl.ANY)
    vector = pltpu.VMEM((2, toks, lanes), f32)
    return pl.pallas_call(
        functools.partial(layer_kernel, features),
        out_shape=(
            jax.ShapeDtypeStruct((toks, cols), bf16),
            jax.ShapeDtypeStruct((toks, features), bf16),
            jax.ShapeDtypeStruct((rows, cols), f32),
        ),
        in_specs=[any_space] * 3,
        out_specs=(any_space,) * 3,
        scratch_shapes=[
            pltpu.VMEM((2, blocks, toks, rows), bf16),
            pltpu.VMEM((blocks, rows, cols), bf16),
            pltpu.VMEM((blocks, rows, cols), bf16),
            pltpu.VMEM((2, toks, cols), bf16),
            pltpu.VMEM((2, toks, cols), bf16),
            pltpu.VMEM((2, toks, cols), f32),
            pltpu.VMEM((toks, cols), f32),
            vector, vector, vector, vector, vector,
            pltpu.VMEM((2, 2, max(HA, RA - HA), cols), bf16),
            pltpu.VMEM((4, RB, cols), bf16),
            pltpu.VMEM((2, max(HB, RB - HB), cols), bf16),
            pltpu.VMEM((2, 2, RA, cols), bf16),
            pltpu.VMEM((2, RB, cols), bf16),
            pltpu.VMEM((RA, cols), bf16),
            pltpu.SemaphoreType.DMA((72,)),
            pltpu.SemaphoreType.DMA((72,)),
            pltpu.SemaphoreType.DMA((32,)),
        ],
        compiler_params=pltpu.CompilerParams(
            collective_id=0, has_side_effects=True, vmem_limit_bytes=62 * 1024 * 1024
        ),
        cost_estimate=pl.CostEstimate(
            flops=6 * toks * features * cols, bytes_accessed=400 * 1024 * 1024, transcendentals=0
        ),
        name="layer",
    )(tokens, gained, cotangent)


def on_device(
    tokens, kv_weight, norm_gain, cotangent, global_params, momentum, local_params, fragment_order
):
    gain = norm_gain[0].astype(f32)[:, None]
    weight = kv_weight[0].astype(f32)
    gained = (weight * gain).astype(bf16)
    fragment_slot = fragment_order[0]
    current = lax.dynamic_index_in_dim(global_params, fragment_slot, 0, keepdims=False)
    moment_old = lax.dynamic_index_in_dim(momentum, fragment_slot, 0, keepdims=False)
    drifted = current - local_params[0]
    replicas = lax.axis_size("replica")
    summed = lax.psum(drifted.astype(bf16), "replica").astype(f32)
    keys_values, input_grad, products = layer(tokens, gained, cotangent)
    weight_share = gain * products
    gain_share = jnp.sum(weight * products, axis=1)
    averaged = summed / replicas
    moment = outer_beta * moment_old + averaged
    updated = current - outer_rate * (averaged + outer_beta * moment)
    new_params = lax.dynamic_update_index_in_dim(global_params, updated, fragment_slot, 0)
    new_momentum = lax.dynamic_update_index_in_dim(momentum, moment, fragment_slot, 0)
    return (keys_values, input_grad, weight_share[None], gain_share[None], new_params, new_momentum)


def solution(mesh):
    return jax.shard_map(
        on_device,
        mesh=mesh,
        in_specs=(
            P(("replica", "fsdp"), None),
            P("replica", "fsdp", None),
            P("replica", "fsdp"),
            P(("replica", "fsdp"), None),
            P(None, "fsdp", None),
            P(None, "fsdp", None),
            P("replica", "fsdp", None),
            P(),
        ),
        out_specs=(
            P(("replica", "fsdp"), None),
            P(("replica", "fsdp"), None),
            P("replica", "fsdp", None),
            P("replica", "fsdp"),
            P(None, "fsdp", None),
            P(None, "fsdp", None),
        ),
        check_vma=False,
    )
```

time: 435 us -> 155 us (0.36)
  waiting for transfers between devices: 247 us -> 0.04 us
  Pallas kernels: 0 us -> 120 us
  blocking collectives: 90.7 us -> 0 us
  matrix products: 50.5 us -> 0 us
  other arithmetic: 24.6 us -> 8.42 us
  local copies, waits for them, and re-layouts: 3.2 us -> 12.7 us
    pallas_call x0 -> x1, Pallas kernels: none -> 120 us  [layer(): pl.pallas_call(functools.partial(layer_kernel, features), out_shape=(jax....]
    reduce_scatter x1 -> x0, waiting for transfers between devices: 112 us -> none  [on_device(): lax.psum_scatter(grad_rows.astype(jnp.bfloat16), 'fsdp', scatter_dimensio...]
    all_gather x1 -> x0, waiting for transfers between devices: 107 us -> none  [on_device(): lax.all_gather(kv_weight, 'fsdp', axis=1, tiled=True)]
    unnamed x1 -> x0, blocking collectives: 65.3 us -> none
    dot_general x3 -> x0, matrix products: 50.5 us -> none  [the longest x1 18.3 us: advance(): jnp.einsum('tc,nc->tn', cotangent, weight_piece, preferred_element_type=j...]
    psum x1, waiting for transfers between devices: 27 us -> 0.02 us  [on_device(): summed = lax.psum(drifted.astype(bf16), 'replica').astype(f32)]
    all_gather x1 -> x0, blocking collectives: 25.4 us -> none  [on_device(): lax.all_gather(norm_gain, 'fsdp', axis=1, tiled=True)]
    convert_element_type x2 -> x3, other arithmetic: 14 us -> 1.9 us  [the longest x1 1.21 us: on_device(): gained = (weight * gain).astype(bf16)]
  transfers between devices with their start and end apart: 3 -> 1, of which waited for: 3 -> 0; matrix products, arithmetic and copies ran while one was open for 6% -> 4% of each run, Pallas kernels for 0% -> 77%
where the time goes in v1:
time: 155 us
  Pallas kernels  120 us (77%)
  between operations  14.3 us (9%)
  local copies, waits for them, and re-layouts  12.7 us (8%)
  other arithmetic  8.42 us (5%)
    pallas_call x1, Pallas kernels, layer(): pl.pallas_call(functools.partial(layer_kernel, features), out_shape=(jax....  120 us
    unnamed x22, local copies, waits for them, and re-layouts  11.6 us
    reduce_sum x1, other arithmetic, on_device(): gain_share = jnp.sum(weight * products, axis=1)  3.86 us
  transfers between devices with their start and end apart: 1, of which 0 were waited for; matrix products, arithmetic and copies ran while one was open for 4% of the time, Pallas kernels for 77%

profile of v1, /device:TPU:0, one launch (start us, length us, event | category | flops | bytes accessed | tf_op | source)
XLA Modules:
  0.0 155.3 jit_solution(7612751355747480554)
XLA Ops:
  7.2 0.0 copy-start
  7.2 0.0 copy-start.4
  7.2 0.0 copy-start.7
  7.2 0.0 copy-start.6
  7.2 0.0 copy-start.8
  7.2 0.0 all-reduce.2.cloned.1.call-start
  7.3 1.4 copy.21
  8.6 0.3 copy-done.4
  8.9 1.0 copy.22
  9.9 0.0 copy-done.8
  10.0 0.2 copy-done.1
  10.2 0.7 fusion.2
  10.9 0.0 all-reduce.2.cloned.1.call-update
  11.0 0.0 copy-done
  11.0 1.2 fusion.gw_hbm
  12.2 119.8 %layer.1 = (bf16[512,1024]{1,0:T(8,128)(2,1)}, bf16[512,8192]{1,0:T(8,128)(2,1)}, f32[512,1024]{1,0:T(8,128)}) custom-call(bf16[512,8192]{1,0:T(8,128)(2,1)} %tok_hbm.1, bf16[512,1024]{1,0:T(8,128)(2,1)} %fusion.gw_hbm, bf16[512,1024]{1,0:T(8,128)(2,1)} %cot_hbm.1), custom_call_target="tpu_custom_call" | custom-call | flops 25769803776 | bytes 419430400 | tf_op jit(solution)/shard_map/layer/pallas_call | solution.py:365
  132.0 0.0 copy-start.2
  132.0 3.9 %fusion.1 = (f32[512]{0:T(512)}, f32[1,512,1024]{2,1,0:T(8,128)}) fusion(f32[512,1024]{1,0:T(8,128)} %get-tuple-element.11, bf16[1,512,1024]{2,1,0:T(8,128)(2,1)S(1)} %copy-done, f32[512]{0:T(512)S(1)} %bitcast.28), kind=kLoop, calls=%fused_computation.3 | loop fusion | flops 2096640 | bytes 5246976 | tf_op jit(solution)/shard_map/reduce_sum | solution.py:417
  135.9 1.1 constant_dynamic-slice_fusion
  136.9 0.0 all-reduce.2.cloned.1.call-done
  137.0 0.9 bitcast_add_fusion
  137.9 1.7 %bitcast_dynamic-update-slice_fusion = (f32[4,64,1024]{2,1,0:T(8,128)S(1)}, f32[4,64,1024]{2,1,0:T(8,128)}) fusion(f32[4,64,1024]{2,1,0:T(8,128)S(1)} %copy-done.2, s32[]{:T(128)S(6)} %select_n.8, f32[64,1024]{1,0:T(8,128)S(1)} %bitcast_add_fusion, f32[4,64,1024]{2,1,0:T(8,128)} %copy-done.1, bf16[64,1024]{1,0:T(8,128)(2,1)} %all-reduce.2.cloned.1.call-done, ...), kind=kLoop, calls=%fused_computation.5 | loop fusion | flops 524288 | bytes 1441796 | tf_op jit(solution)/shard_map/jit(dynamic_update_index_in_dim)/dynamic_update_slice | solution.py:422
  139.6 1.0 copy.23
  140.6 7.8 %copy.24 = bf16[512,8192]{1,0:T(8,128)(2,1)} copy(bf16[512,8192]{1,0:T(8,128)(2,1)} %get-tuple-element.23) | data formatting | bytes 16777216
  (9 shorter events, 0.0 us)
Async XLA Ops:
  7.2 3.8 %copy-start = (bf16[1,512,1024]{2,1,0:T(8,128)(2,1)S(1)}, bf16[1,512,1024]{2,1,0:T(8,128)(2,1)}, u32[]{:S(2)}) copy-start(bf16[1,512,1024]{2,1,0:T(8,128)(2,1)} %param.9) | copy-start | bytes 3145732
  7.2 1.7 %copy-start.4 = (f32[4,64,1024]{2,1,0:T(8,128)S(1)}, f32[4,64,1024]{2,1,0:T(8,128)}, u32[]{:S(2)}) copy-start(f32[4,64,1024]{2,1,0:T(8,128)} %param.13) | copy-start | bytes 3145732
  7.2 3.7 %copy-start.7 = (bf16[1,512]{1,0:T(2,128)(2,1)S(1)}, bf16[1,512]{1,0:T(2,128)(2,1)}, u32[]{:S(2)}) copy-start(bf16[1,512]{1,0:T(2,128)(2,1)} %param.10) | copy-start | bytes 3076
  7.2 3.0 %copy-start.6 = (f32[1,64,1024]{2,1,0:T(8,128)S(1)}, f32[1,64,1024]{2,1,0:T(8,128)}, u32[]{:S(2)}) copy-start(f32[1,64,1024]{2,1,0:T(8,128)} %param.14) | copy-start | bytes 786436
  7.2 2.7 %copy-start.8 = (s32[4]{0:T(128)S(1)}, s32[4]{0:T(128)}, u32[]{:S(2)}) copy-start(s32[4]{0:T(128)} %param.15) | copy-start | bytes 52
  7.2 129.7 %all-reduce.2.cloned.1.call-start = ((), (), s32[]{:S(2)}) async-start(), calls=%async_computation | async-start | bytes 262144 | tf_op jit(solution)/shard_map/psum | solution.py:414
  8.9 1.3 copy-start.1
  132.0 5.0 %copy-start.2 = (f32[4,64,1024]{2,1,0:T(8,128)S(1)}, f32[4,64,1024]{2,1,0:T(8,128)}, u32[]{:S(2)}) copy-start(f32[4,64,1024]{2,1,0:T(8,128)} %copy.22) | copy-start | bytes 3145732
  135.9 3.8 %copy-start.5 = (bf16[512,1024]{1,0:T(8,128)(2,1)S(1)}, bf16[512,1024]{1,0:T(8,128)(2,1)}, u32[]{:S(2)}) copy-start(bf16[512,1024]{1,0:T(8,128)(2,1)} %get-tuple-element.22) | copy-start | bytes 3145732
  139.6 8.8 %copy-start.3 = (f32[4,64,1024]{2,1,0:T(8,128)}, f32[4,64,1024]{2,1,0:T(8,128)S(1)}, u32[]{:S(2)}) copy-start(f32[4,64,1024]{2,1,0:T(8,128)S(1)} %get-tuple-element.27) | copy-start | bytes 3145732
Sparse Core Ops, SparseCore 0:
  11.1 76.5 all-reduce.1

commit v2 on v1

--- a/solution.py
+++ b/solution.py
@@ -22,11 +22,13 @@
 
 
 def layer_kernel(
-    features, tok_hbm, gw_hbm, cot_hbm, kv_out, ig_out, u_out,
+    features, order, gain, tok_hbm, w_hbm, cot_hbm, outer_hbm, inner_hbm,
+    kv_out, ig_out, u_out, drift_out,
     tok, w, u, cot, cots, kvp, kvx, sq, sq_in, inv, rs, rs_in,
-    ra_opp, rb_z, rb_opp, ra_x, rb_x, ra_z, send_sem, recv_sem, local_sem,
+    ra_opp, rb_z, rb_opp, ra_x, rb_x, ra_z,
+    outer, inner, drift, drift_in, drifts, drifts_in, send_sem, recv_sem, local_sem,
 ):
-    rows, cols = gw_hbm.shape
+    rows, cols = w_hbm.shape
     toks = tok_hbm.shape[0]
     RA, RB, HA, HB = split_rows(rows)
     r = lax.axis_index("replica")
@@ -42,14 +44,38 @@
     left = at(zh, lax.rem(x + 3, 4), c)
     partner = at(1 - zh, x, c)
     sibling = at(zh, x, 1 - c)
+    z_lo, y = lax.div(r, 4), lax.rem(r, 4)
+    peers = (
+        ((1 - z_lo) * 4 + y, me),
+        (z_lo * 4 + y + 1 - 2 * lax.rem(y, 2), me),
+        (z_lo * 4 + 3 - y, me),
+    )
 
     def slot(plane, dx):
         return (zh if plane == 0 else 1 - zh) * 4 + lax.rem(x + dx + 4, 4)
 
+    blocks = features // rows // 2
+
+    def columns(k, core):
+        return pl.ds(pl.multiple_of((2 * k + core) * rows, rows), rows)
+
     barrier = pltpu.get_barrier_semaphore()
-    for other in (right, left, partner, sibling):
+    around = (right, left, partner, sibling, *peers)
+    for other in around:
         pl.semaphore_signal(barrier, inc=1, device_id=other, device_id_type=MESH)
-    pl.semaphore_wait(barrier, 4)
+    early = 2 * blocks + 5
+
+    def load(src, dst, i):
+        copy = pltpu.make_async_copy(src, dst, local_sem.at[i])
+        copy.start()
+        return copy
+
+    load_w = load(w_hbm, cots.at[0], early)
+    loads = [load(tok_hbm.at[:, columns(k, c)], tok.at[0, k], k) for k in range(blocks)]
+    load_cot = load(cot_hbm, cot.at[0], blocks)
+    load_outer = load(outer_hbm, outer, early + 2)
+    load_inner = load(inner_hbm, inner, early + 3)
+    pl.semaphore_wait(barrier, len(around))
 
     sent = {}
 
@@ -71,31 +97,47 @@
     b_first, b_last = pl.ds(RA, HB), pl.ds(RA + HB, RB - HB)
 
     own = slot(0, 0)
-    send("g_right_b", gw_hbm.at[b_rows], w.at[own, b_rows], right)
-    send("g_left_b", gw_hbm.at[b_rows], w.at[own, b_rows], left)
-    send("g_z_a", gw_hbm.at[a_rows], w.at[own, a_rows], partner)
-    send("g_right_a", gw_hbm.at[a_rows], w.at[own, a_rows], right)
-    send("g_left_a", gw_hbm.at[a_rows], w.at[own, a_rows], left)
-    send("g_z_b", gw_hbm.at[b_rows], w.at[own, b_rows], partner)
-
-    def columns(k, core):
-        return pl.ds(pl.multiple_of((2 * k + core) * rows, rows), rows)
-
-    blocks = features // rows // 2
-    loads = []
+    lanes = min(LANES, rows)
+    AT = 16
+
+    def wide(column, width):
+        return jnp.concatenate([column] * (width // lanes), axis=1) if width > lanes else column[:, :width]
+
+    def gained(lo, count):
+        @pl.loop(0, count // AT)
+        def _(i):
+            to = pl.ds(pl.multiple_of(lo + i * AT, AT), AT)
+            w[own, to, :] = (cots[0, to, :].astype(f32) * wide(rs[0, to, :], cols)).astype(bf16)
+
+    rs[0, pl.ds(0, rows), :] = jnp.broadcast_to(gain[...].astype(f32), (lanes, rows)).T
+    load_w.wait()
+    gained(RA, RB)
+    send("g_right_b", w.at[own, b_rows], w.at[own, b_rows], right)
+    send("g_left_b", w.at[own, b_rows], w.at[own, b_rows], left)
+    gained(0, RA)
+    send("g_z_a", w.at[own, a_rows], w.at[own, a_rows], partner)
+    send("g_right_a", w.at[own, a_rows], w.at[own, a_rows], right)
+    send("g_left_a", w.at[own, a_rows], w.at[own, a_rows], left)
+    send("g_z_b", w.at[own, b_rows], w.at[own, b_rows], partner)
     for k in range(blocks):
-        load = pltpu.make_async_copy(tok_hbm.at[:, columns(k, c)], tok.at[0, k], local_sem.at[k])
-        load.start()
-        loads.append(load)
         send(f"t{k}", tok_hbm.at[:, columns(k, 1 - c)], tok.at[1, k], sibling)
-    load_cot = pltpu.make_async_copy(cot_hbm, cot.at[0], local_sem.at[blocks])
-    load_cot.start()
     send("cot", cot_hbm, cot.at[1], sibling)
-    load_w = pltpu.make_async_copy(gw_hbm, w.at[own], local_sem.at[blocks + 1])
-    load_w.start()
+
+    load_outer.wait()
+    load_inner.wait()
+    drift[...] = (outer[order[0]] - inner[...]).astype(bf16)
+    send("d0", drift, drift_in, peers[0])
+
+    def drift_step(step):
+        got(f"d{step}")
+        if step == 0:
+            drifts[0] = drift[...].astype(f32) + drift_in[...].astype(f32)
+        else:
+            drifts[step] = drifts[step - 1] + drifts_in[step - 1]
+        if step < 2:
+            send(f"d{step + 1}", drifts.at[step], drifts_in.at[step], peers[step + 1])
 
     RT = min(64, toks)
-    lanes = min(LANES, rows)
 
     def square_block(half, k, fresh):
         @pl.loop(0, toks // RT)
@@ -121,9 +163,6 @@
     send("sq", sq, sq_in, sibling)
     load_cot.wait()
     got("cot", "sq")
-
-    def wide(column, width):
-        return jnp.concatenate([column] * (width // lanes), axis=1) if width > lanes else column[:, :width]
 
     for half in range(2):
         @pl.loop(0, toks // RT)
@@ -197,8 +236,6 @@
             ig_store(k).start()
             ig_send(k).start()
 
-    AT = 16
-
     def add_rows(count, dst, dst_at, *srcs):
         @pl.loop(0, count // AT)
         def _(i):
@@ -248,17 +285,20 @@
     send("h_right_a", w.at[far, a_rows], w.at[far, a_rows], right)
     send("h_left_a", w.at[far, a_rows], w.at[far, a_rows], left)
     u_loop(0, 3)
+    drift_step(0)
     got("g_right_a", "g_left_a")
     send("g2_right_a", w.at[mine_l, a_first], w.at[mine_l, a_first], right)
     send("g2_left_a", w.at[mine_r, a_last], w.at[mine_r, a_last], left)
     u_loop(3, 6)
+    drift_step(1)
     got("g2_right_b", "g2_left_b")
     send("gz_o", w.at[mine_o, b_rows], w.at[mine_o, b_rows], partner)
     u_loop(6, 8)
     for j, dx in enumerate((2, 1, -1, 0)):
         send(f"rz{j}", u.at[slot(1, dx), b_rows], rb_z.at[j], partner)
-    load_w.wait()
     kv_block(own, True)
+    drift_step(2)
+    store_drift = load(drifts.at[2], drift_out, early)
 
     @pl.loop(0, 2)
     def _(i):
@@ -350,13 +390,14 @@
         ig_store(k).wait()
         ig_send(k).wait()
 
+    store_drift.wait()
     last_b.wait()
     last_a.wait()
 
 
-def layer(tokens, gained, cotangent):
+def layer(tokens, weight, gain, cotangent, outer, inner, order):
     toks, features = tokens.shape
-    rows, cols = gained.shape
+    rows, cols = weight.shape
     blocks = features // rows // 2
     RA, RB, HA, HB = split_rows(rows)
     lanes = min(LANES, rows)
@@ -368,9 +409,11 @@
             jax.ShapeDtypeStruct((toks, cols), bf16),
             jax.ShapeDtypeStruct((toks, features), bf16),
             jax.ShapeDtypeStruct((rows, cols), f32),
+            jax.ShapeDtypeStruct(inner.shape, f32),
         ),
-        in_specs=[any_space] * 3,
-        out_specs=(any_space,) * 3,
+        in_specs=[pl.BlockSpec(memory_space=pltpu.SMEM), pl.BlockSpec(memory_space=pltpu.VMEM)]
+        + [any_space] * 5,
+        out_specs=(any_space,) * 4,
         scratch_shapes=[
             pltpu.VMEM((2, blocks, toks, rows), bf16),
             pltpu.VMEM((blocks, rows, cols), bf16),
@@ -386,41 +429,139 @@
             pltpu.VMEM((2, 2, RA, cols), bf16),
             pltpu.VMEM((2, RB, cols), bf16),
             pltpu.VMEM((RA, cols), bf16),
+            pltpu.VMEM(outer.shape, f32),
+            pltpu.VMEM(inner.shape, f32),
+            pltpu.VMEM(inner.shape, bf16),
+            pltpu.VMEM(inner.shape, bf16),
+            pltpu.VMEM((3, *inner.shape), f32),
+            pltpu.VMEM((2, *inner.shape), f32),
             pltpu.SemaphoreType.DMA((72,)),
             pltpu.SemaphoreType.DMA((72,)),
             pltpu.SemaphoreType.DMA((32,)),
         ],
         compiler_params=pltpu.CompilerParams(
-            collective_id=0, has_side_effects=True, vmem_limit_bytes=62 * 1024 * 1024
+            collective_id=0, has_side_effects=True, vmem_limit_bytes=60 * 1024 * 1024
         ),
         cost_estimate=pl.CostEstimate(
             flops=6 * toks * features * cols, bytes_accessed=400 * 1024 * 1024, transcendentals=0
         ),
         name="layer",
-    )(tokens, gained, cotangent)
+    )(order, gain, tokens, weight, cotangent, outer, inner)
+
+
+PIECES = 8
+
+
+def finish_kernel(
+    replicas, order, gain, ig_in, kv_in, u_in, drift_in, w_in, outer_in, moment_in,
+    kv_out, ig_out, wg_out, gg_out, outer_out, moment_out,
+    ig, kv, u, w, column, partial, share, drift, outer, moment, sem,
+):
+    rows, cols = u.shape
+    lanes = min(LANES, rows)
+    started = []
+
+    def copy(src, dst):
+        move = pltpu.make_async_copy(src, dst, sem.at[len(started)])
+        move.start()
+        started.append(move)
+        return move
+
+    get_u, get_w = copy(u_in, u), copy(w_in, w)
+    get_drift, get_outer, get_moment = copy(drift_in, drift), copy(outer_in, outer), copy(moment_in, moment)
+    step = ig_in.shape[0] // PIECES
+    pieces = [pl.ds(i * step, step) for i in range(PIECES)]
+    gets = [copy(kv_in, kv)] + [copy(ig_in.at[p], ig.at[p]) for p in pieces]
+    puts = [(kv, kv_out)] + [(ig.at[p], ig_out.at[p]) for p in pieces]
+    moves = []
+
+    def pass_on(count):
+        for _ in range(count):
+            gets.pop(0).wait()
+            moves.append(copy(*puts.pop(0)))
+
+    column[...] = jnp.broadcast_to(gain[...].astype(f32), (lanes, rows)).T
+    get_u.wait()
+    get_w.wait()
+    RT = 32
+
+    @pl.loop(0, rows // RT)
+    def _(i):
+        at_rows = pl.ds(pl.multiple_of(i * RT, RT), RT)
+        whole = u[at_rows, :]
+        product = whole * w[at_rows, :].astype(f32)
+        total = product[:, :lanes]
+        for j in range(1, cols // lanes):
+            total = total + product[:, j * lanes : (j + 1) * lanes]
+        partial[at_rows, :] = total
+        u[at_rows, :] = whole * jnp.concatenate([column[at_rows, :]] * (cols // lanes), axis=1)
+
+    moves.append(copy(u, wg_out))
+    pass_on(3)
+    share[...] = jnp.sum(partial[...].T, axis=0, keepdims=True)
+    moves.append(copy(share, gg_out))
+    pass_on(2)
+    get_drift.wait()
+    get_outer.wait()
+    get_moment.wait()
+    now = order[0]
+    averaged = drift[...] / replicas
+    fresh = outer_beta * moment[now] + averaged
+    moment[now] = fresh
+    outer[now] = outer[now] - outer_rate * (averaged + outer_beta * fresh)
+    moves.append(copy(moment, moment_out))
+    moves.append(copy(outer, outer_out))
+    pass_on(len(gets))
+    for move in moves:
+        move.wait()
+
+
+def finish(replicas, order, ig, kv, u, drift, weight, gain, outer, moment):
+    rows, cols = u.shape
+    lanes = min(LANES, rows)
+    any_space = pl.BlockSpec(memory_space=pl.ANY)
+    return pl.pallas_call(
+        functools.partial(finish_kernel, replicas),
+        out_shape=(
+            jax.ShapeDtypeStruct(kv.shape, bf16),
+            jax.ShapeDtypeStruct(ig.shape, bf16),
+            jax.ShapeDtypeStruct(u.shape, f32),
+            jax.ShapeDtypeStruct(gain.shape, f32),
+            jax.ShapeDtypeStruct(outer.shape, f32),
+            jax.ShapeDtypeStruct(moment.shape, f32),
+        ),
+        in_specs=[pl.BlockSpec(memory_space=pltpu.SMEM), pl.BlockSpec(memory_space=pltpu.VMEM)]
+        + [any_space] * 7,
+        out_specs=(any_space,) * 6,
+        scratch_shapes=[
+            pltpu.VMEM(ig.shape, bf16),
+            pltpu.VMEM(kv.shape, bf16),
+            pltpu.VMEM((rows, cols), f32),
+            pltpu.VMEM((rows, cols), bf16),
+            pltpu.VMEM((rows, lanes), f32),
+            pltpu.VMEM((rows, lanes), f32),
+            pltpu.VMEM(gain.shape, f32),
+            pltpu.VMEM(drift.shape, f32),
+            pltpu.VMEM(outer.shape, f32),
+            pltpu.VMEM(moment.shape, f32),
+            pltpu.SemaphoreType.DMA((32,)),
+        ],
+        compiler_params=pltpu.CompilerParams(vmem_limit_bytes=60 * 1024 * 1024),
+        name="finish",
+    )(order, gain, ig, kv, u, drift, weight, outer, moment)
 
 
 def on_device(
     tokens, kv_weight, norm_gain, cotangent, global_params, momentum, local_params, fragment_order
 ):
-    gain = norm_gain[0].astype(f32)[:, None]
-    weight = kv_weight[0].astype(f32)
-    gained = (weight * gain).astype(bf16)
-    fragment_slot = fragment_order[0]
-    current = lax.dynamic_index_in_dim(global_params, fragment_slot, 0, keepdims=False)
-    moment_old = lax.dynamic_index_in_dim(momentum, fragment_slot, 0, keepdims=False)
-    drifted = current - local_params[0]
-    replicas = lax.axis_size("replica")
-    summed = lax.psum(drifted.astype(bf16), "replica").astype(f32)
-    keys_values, input_grad, products = layer(tokens, gained, cotangent)
-    weight_share = gain * products
-    gain_share = jnp.sum(weight * products, axis=1)
-    averaged = summed / replicas
-    moment = outer_beta * moment_old + averaged
-    updated = current - outer_rate * (averaged + outer_beta * moment)
-    new_params = lax.dynamic_update_index_in_dim(global_params, updated, fragment_slot, 0)
-    new_momentum = lax.dynamic_update_index_in_dim(momentum, moment, fragment_slot, 0)
-    return (keys_values, input_grad, weight_share[None], gain_share[None], new_params, new_momentum)
+    weight = kv_weight[0]
+    kv, ig, u, drift = layer(
+        tokens, weight, norm_gain, cotangent, global_params, local_params[0], fragment_order
+    )
+    keys_values, input_grad, weight_grad, gain_grad, new_params, new_momentum = finish(
+        lax.axis_size("replica"), fragment_order, ig, kv, u, drift, weight, norm_gain, global_params, momentum
+    )
+    return (keys_values, input_grad, weight_grad[None], gain_grad, new_params, new_momentum)
 
 
 def solution(mesh):

time: 155 us -> 133 us (0.86)
  between operations: 14.3 us -> 0.64 us
  Pallas kernels: 120 us -> 133 us
  local copies, waits for them, and re-layouts: 12.7 us -> 0 us
  other arithmetic: 8.42 us -> 0 us
    unnamed x22 -> x0, local copies, waits for them, and re-layouts: 11.6 us -> none
    pallas_call x0 -> x1, Pallas kernels: none -> 11 us  [finish(): pl.pallas_call(functools.partial(finish_kernel, replicas), out_shape=(jax...]
    reduce_sum x1 -> x0, other arithmetic: 3.86 us -> none  [on_device(): gain_share = jnp.sum(weight * products, axis=1)]
    convert_element_type x3 -> x0, other arithmetic: 1.9 us -> none  [the longest x1 1.21 us: on_device(): gained = (weight * gain).astype(bf16)]
    pallas_call x1, Pallas kernels: 120 us -> 122 us  [layer(): pl.pallas_call(functools.partial(layer_kernel, features), out_shape=(jax....]
    dynamic_update_slice x1 -> x0, other arithmetic: 1.71 us -> none  [on_device(): lax.dynamic_update_index_in_dim(momentum, moment, fragment_slot, 0)]
  transfers between devices with their start and end apart: 1 -> 0, of which waited for: 0 -> 0; matrix products, arithmetic and copies ran while one was open for 4% -> 0% of each run, Pallas kernels for 77% -> 0%
where the time goes in v2:
time: 133 us
  Pallas kernels  133 us (100%)
    pallas_call x1, Pallas kernels, layer(): pl.pallas_call(functools.partial(layer_kernel, features), out_shape=(jax....  122 us
    pallas_call x1, Pallas kernels, finish(): pl.pallas_call(functools.partial(finish_kernel, replicas), out_shape=(jax...  11 us

profile of v2, /device:TPU:0, one launch (start us, length us, event | category | flops | bytes accessed | tf_op | source)
XLA Modules:
  0.0 133.2 jit_solution(3046935351443047946)
XLA Ops:
  0.6 121.6 %layer.1 = (bf16[512,1024]{1,0:T(8,128)(2,1)}, bf16[512,8192]{1,0:T(8,128)(2,1)}, f32[512,1024]{1,0:T(8,128)}, f32[64,1024]{1,0:T(8,128)}) custom-call(s32[4]{0:T(128)} %order.3, bf16[1,512]{1,0:T(2,128)(2,1)} %gain.3, bf16[512,8192]{1,0:T(8,128)(2,1)} %tok_hbm.1, bf16[512,1024]{1,0:T(8,128)(2,1)} %bitcast.3, bf16[512,1024]{1,0:T(8,128)(2,1)} %cot_hbm.1, ...), custom_call_target="tpu_custom_call" | custom-call | flops 25769803776 | bytes 419430400 | tf_op jit(solution)/shard_map/layer/pallas_call | solution.py:406
  122.2 11.0 %finish.1 = (bf16[512,1024]{1,0:T(8,128)(2,1)}, bf16[512,8192]{1,0:T(8,128)(2,1)}, f32[512,1024]{1,0:T(8,128)}, f32[1,512]{1,0:T(1,128)}, f32[4,64,1024]{2,1,0:T(8,128)}, /*index=5*/f32[4,64,1024]{2,1,0:T(8,128)}) custom-call(s32[4]{0:T(128)} %order.3, bf16[1,512]{1,0:T(2,128)(2,1)} %gain.3, bf16[512,8192]{1,0:T(8,128)(2,1)} %get-tuple-element.16.ig_in, ...), custom_call_target="tpu_custom_call" | custom-call | tf_op jit(solution)/shard_map/finish/pallas_call | solution.py:523

commit v3 on v2

--- a/solution.py
+++ b/solution.py
@@ -23,9 +23,9 @@
 
 def layer_kernel(
     features, order, gain, tok_hbm, w_hbm, cot_hbm, outer_hbm, inner_hbm,
-    kv_out, ig_out, u_out, drift_out,
+    kv_out, ig_out, own_out, xa_out, za_out, xb_out, drift_out,
     tok, w, u, cot, cots, kvp, kvx, sq, sq_in, inv, rs, rs_in,
-    ra_opp, rb_z, rb_opp, ra_x, rb_x, ra_z,
+    ra_opp, rb_z, rb_opp, ra_x,
     outer, inner, drift, drift_in, drifts, drifts_in, send_sem, recv_sem, local_sem,
 ):
     rows, cols = w_hbm.shape
@@ -126,16 +126,36 @@
     load_outer.wait()
     load_inner.wait()
     drift[...] = (outer[order[0]] - inner[...]).astype(bf16)
-    send("d0", drift, drift_in, peers[0])
+    n_half, n_quarter = drift.shape[0] // 2, drift.shape[0] // 4
+    keep = lax.rem(y + lax.div(y, 2), 2)
+    upper = lax.div(y, 2)
+    half_at = pl.multiple_of(keep * n_half, n_half)
+    quarter_at = pl.multiple_of(half_at + upper * n_quarter, n_quarter)
+    my_half, my_quarter = pl.ds(half_at, n_half), pl.ds(quarter_at, n_quarter)
+    other_half = pl.ds(pl.multiple_of((1 - keep) * n_half, n_half), n_half)
+    other_quarter = pl.ds(pl.multiple_of(half_at + (1 - upper) * n_quarter, n_quarter), n_quarter)
+    send("d0", drift.at[other_half], drift_in.at[pl.ds(0, n_half)], peers[1])
 
     def drift_step(step):
         got(f"d{step}")
         if step == 0:
-            drifts[0] = drift[...].astype(f32) + drift_in[...].astype(f32)
-        else:
-            drifts[step] = drifts[step - 1] + drifts_in[step - 1]
-        if step < 2:
-            send(f"d{step + 1}", drifts.at[step], drifts_in.at[step], peers[step + 1])
+            mine_in = pl.ds(pl.multiple_of(upper * n_quarter, n_quarter), n_quarter)
+            other_in = pl.ds(pl.multiple_of((1 - upper) * n_quarter, n_quarter), n_quarter)
+            drifts[my_quarter, :] = drift[my_quarter, :].astype(f32) + drift_in[mine_in, :].astype(f32)
+            drifts_in[0] = drift[other_quarter, :].astype(f32) + drift_in[other_in, :].astype(f32)
+            send("d1", drifts_in.at[0], drifts_in.at[1], peers[2])
+        elif step == 1:
+            total = (drifts[my_quarter, :] + drifts_in[1]).astype(bf16)
+            drift_in[pl.ds(n_half, n_quarter), :] = total
+            send("d2", drift_in.at[pl.ds(n_half, n_quarter)], drift_in.at[pl.ds(n_half + n_quarter, n_quarter)], peers[0])
+        elif step == 2:
+            drifts[my_quarter, :] = (
+                drift_in[pl.ds(n_half, n_quarter), :].astype(f32)
+                + drift_in[pl.ds(n_half + n_quarter, n_quarter), :].astype(f32)
+            )
+            send("d3", drifts.at[my_quarter], drifts.at[my_quarter], peers[2])
+        elif step == 3:
+            send("d4", drifts.at[my_half], drifts.at[my_half], peers[1])
 
     RT = min(64, toks)
 
@@ -249,9 +269,10 @@
         got(f"ro_r{plane}", f"ro_l{plane}")
         to_right, to_left = slot(plane, 1), slot(plane, -1)
         add_rows(HA, to_right, 0, (ra_opp, (0, plane)))
-        send(f"ra_r{plane}", u.at[to_right, a_rows], ra_x.at[0, plane], right)
+        land = xa_out if plane == 0 else ra_x
+        send(f"ra_r{plane}", u.at[to_right, a_rows], land.at[0], right)
         add_rows(RA - HA, to_left, HA, (ra_opp, (1, plane)))
-        send(f"ra_l{plane}", u.at[to_left, a_rows], ra_x.at[1, plane], left)
+        send(f"ra_l{plane}", u.at[to_left, a_rows], land.at[1], left)
 
     def reduce_b_opposite():
         got("rz0")
@@ -266,9 +287,9 @@
     def reduce_b_side():
         got("rbo_r", "rbo_l")
         add_rows(HB, mine_r, RA, (rb_opp, (0,)))
-        send("rb_r", u.at[mine_r, b_rows], rb_x.at[0], right)
+        send("rb_r", u.at[mine_r, b_rows], xb_out.at[0], right)
         add_rows(RB - HB, mine_l, RA + HB, (rb_opp, (1,)))
-        send("rb_l", u.at[mine_l, b_rows], rb_x.at[1], left)
+        send("rb_l", u.at[mine_l, b_rows], xb_out.at[1], left)
 
     def u_loop(lo, hi):
         @pl.loop(lo, hi)
@@ -298,7 +319,6 @@
         send(f"rz{j}", u.at[slot(1, dx), b_rows], rb_z.at[j], partner)
     kv_block(own, True)
     drift_step(2)
-    store_drift = load(drifts.at[2], drift_out, early)
 
     @pl.loop(0, 2)
     def _(i):
@@ -311,6 +331,7 @@
         opp = slot(plane, 2)
         send(f"ro_r{plane}", u.at[opp, a_first], ra_opp.at[0, plane, pl.ds(0, HA)], right)
         send(f"ro_l{plane}", u.at[opp, a_last], ra_opp.at[1, plane, pl.ds(0, RA - HA)], left)
+    drift_step(3)
     got("g2_right_a", "g2_left_a", "g_z_b")
     kv_block(mine_o)
     kv_block(far)
@@ -332,6 +353,8 @@
             rs[half, at_rows, :] = total
 
     send("rs", rs, rs_in, sibling)
+    got("d4")
+    store_drift = load(drifts, drift_out, early)
     reduce_a(1)
     sent["sq"].wait_send()
     got("rs", "kv")
@@ -353,34 +376,17 @@
     reduce_b_opposite()
     reduce_a(0)
     back_loop(2, 5)
+    got("ra_r1", "ra_l1")
+    add_rows(RA, far, 0, (ra_x, (0,)), (ra_x, (1,)))
+    send("za", u.at[far, a_rows], za_out, partner)
     reduce_b_side()
     back_loop(5, 8)
-    got("ra_r1", "ra_l1")
-    add_rows(RA, far, 0, (ra_x, (0, 1)), (ra_x, (1, 1)))
-    send("za", u.at[far, a_rows], ra_z, partner)
     got("rz3")
     add_rows(RB, own, RA, (rb_z, (3,)))
 
+    store_own = load(u.at[own], own_out, 2 * blocks + 3)
     store_kv.wait()
-
-    def last_sum(lo, count, *srcs):
-        @pl.loop(0, count // AT)
-        def _(i):
-            to = pl.ds(pl.multiple_of(lo + i * AT, AT), AT)
-            total = u[own, to, :].astype(f32)
-            for ref, index in srcs:
-                total = total + ref[(*index, pl.ds(pl.multiple_of(i * AT, AT), AT), slice(None))].astype(f32)
-            kvx[to, :] = total
-        store = pltpu.make_async_copy(
-            kvx.at[pl.ds(lo, count)], u_out.at[pl.ds(lo, count)], local_sem.at[2 * blocks + 3 + (lo > 0)]
-        )
-        store.start()
-        return store
-
-    got("rb_r", "rb_l")
-    last_b = last_sum(RA, RB, (rb_x, (0,)), (rb_x, (1,)))
-    got("ra_r0", "ra_l0", "za")
-    last_a = last_sum(0, RA, (ra_x, (0, 0)), (ra_x, (1, 0)), (ra_z, ()))
+    got("rb_r", "rb_l", "ra_r0", "ra_l0", "za")
     for name, copy in sent.items():
         if name != "sq":
             copy.wait_send()
@@ -391,8 +397,7 @@
         ig_send(k).wait()
 
     store_drift.wait()
-    last_b.wait()
-    last_a.wait()
+    store_own.wait()
 
 
 def layer(tokens, weight, gain, cotangent, outer, inner, order):
@@ -408,12 +413,15 @@
         out_shape=(
             jax.ShapeDtypeStruct((toks, cols), bf16),
             jax.ShapeDtypeStruct((toks, features), bf16),
-            jax.ShapeDtypeStruct((rows, cols), f32),
+            jax.ShapeDtypeStruct((rows, cols), bf16),
+            jax.ShapeDtypeStruct((2, RA, cols), bf16),
+            jax.ShapeDtypeStruct((RA, cols), bf16),
+            jax.ShapeDtypeStruct((2, RB, cols), bf16),
             jax.ShapeDtypeStruct(inner.shape, f32),
         ),
         in_specs=[pl.BlockSpec(memory_space=pltpu.SMEM), pl.BlockSpec(memory_space=pltpu.VMEM)]
         + [any_space] * 5,
-        out_specs=(any_space,) * 4,
+        out_specs=(any_space,) * 7,
         scratch_shapes=[
             pltpu.VMEM((2, blocks, toks, rows), bf16),
             pltpu.VMEM((blocks, rows, cols), bf16),
@@ -426,15 +434,13 @@
             pltpu.VMEM((2, 2, max(HA, RA - HA), cols), bf16),
             pltpu.VMEM((4, RB, cols), bf16),
             pltpu.VMEM((2, max(HB, RB - HB), cols), bf16),
-            pltpu.VMEM((2, 2, RA, cols), bf16),
-            pltpu.VMEM((2, RB, cols), bf16),
-            pltpu.VMEM((RA, cols), bf16),
+            pltpu.VMEM((2, RA, cols), bf16),
             pltpu.VMEM(outer.shape, f32),
             pltpu.VMEM(inner.shape, f32),
             pltpu.VMEM(inner.shape, bf16),
             pltpu.VMEM(inner.shape, bf16),
-            pltpu.VMEM((3, *inner.shape), f32),
-            pltpu.VMEM((2, *inner.shape), f32),
+            pltpu.VMEM(inner.shape, f32),
+            pltpu.VMEM((2, inner.shape[0] // 4, inner.shape[1]), f32),
             pltpu.SemaphoreType.DMA((72,)),
             pltpu.SemaphoreType.DMA((72,)),
             pltpu.SemaphoreType.DMA((32,)),
@@ -453,9 +459,9 @@
 
 
 def finish_kernel(
-    replicas, order, gain, ig_in, kv_in, u_in, drift_in, w_in, outer_in, moment_in,
+    replicas, order, gain, ig_in, kv_in, own_in, xa_in, za_in, xb_in, drift_in, w_in, outer_in, moment_in,
     kv_out, ig_out, wg_out, gg_out, outer_out, moment_out,
-    ig, kv, u, w, column, partial, share, drift, outer, moment, sem,
+    ig, kv, own, xa, za, xb, u, w, column, partial, share, drift, outer, moment, sem,
 ):
     rows, cols = u.shape
     lanes = min(LANES, rows)
@@ -467,7 +473,7 @@
         started.append(move)
         return move
 
-    get_u, get_w = copy(u_in, u), copy(w_in, w)
+    terms = [copy(own_in, own), copy(w_in, w), copy(xa_in, xa), copy(za_in, za), copy(xb_in, xb)]
     get_drift, get_outer, get_moment = copy(drift_in, drift), copy(outer_in, outer), copy(moment_in, moment)
     step = ig_in.shape[0] // PIECES
     pieces = [pl.ds(i * step, step) for i in range(PIECES)]
@@ -481,21 +487,28 @@
             moves.append(copy(*puts.pop(0)))
 
     column[...] = jnp.broadcast_to(gain[...].astype(f32), (lanes, rows)).T
-    get_u.wait()
-    get_w.wait()
+    for term in terms:
+        term.wait()
     RT = 32
-
-    @pl.loop(0, rows // RT)
-    def _(i):
-        at_rows = pl.ds(pl.multiple_of(i * RT, RT), RT)
-        whole = u[at_rows, :]
-        product = whole * w[at_rows, :].astype(f32)
-        total = product[:, :lanes]
-        for j in range(1, cols // lanes):
-            total = total + product[:, j * lanes : (j + 1) * lanes]
-        partial[at_rows, :] = total
-        u[at_rows, :] = whole * jnp.concatenate([column[at_rows, :]] * (cols // lanes), axis=1)
-
+    first = za.shape[0]
+
+    def last_sum(lo, count, *others):
+        @pl.loop(0, count // RT)
+        def _(i):
+            at_rows = pl.ds(pl.multiple_of(lo + i * RT, RT), RT)
+            there = pl.ds(pl.multiple_of(i * RT, RT), RT)
+            whole = own[at_rows, :].astype(f32)
+            for ref, index in others:
+                whole = whole + ref[(*index, there, slice(None))].astype(f32)
+            product = whole * w[at_rows, :].astype(f32)
+            total = product[:, :lanes]
+            for j in range(1, cols // lanes):
+                total = total + product[:, j * lanes : (j + 1) * lanes]
+            partial[at_rows, :] = total
+            u[at_rows, :] = whole * jnp.concatenate([column[at_rows, :]] * (cols // lanes), axis=1)
+
+    last_sum(0, first, (xa, (0,)), (xa, (1,)), (za, ()))
+    last_sum(first, rows - first, (xb, (0,)), (xb, (1,)))
     moves.append(copy(u, wg_out))
     pass_on(3)
     share[...] = jnp.sum(partial[...].T, axis=0, keepdims=True)
@@ -516,8 +529,8 @@
         move.wait()
 
 
-def finish(replicas, order, ig, kv, u, drift, weight, gain, outer, moment):
-    rows, cols = u.shape
+def finish(replicas, order, ig, kv, terms, drift, weight, gain, outer, moment):
+    rows, cols = weight.shape
     lanes = min(LANES, rows)
     any_space = pl.BlockSpec(memory_space=pl.ANY)
     return pl.pallas_call(
@@ -525,17 +538,18 @@
         out_shape=(
             jax.ShapeDtypeStruct(kv.shape, bf16),
             jax.ShapeDtypeStruct(ig.shape, bf16),
-            jax.ShapeDtypeStruct(u.shape, f32),
+            jax.ShapeDtypeStruct((rows, cols), f32),
             jax.ShapeDtypeStruct(gain.shape, f32),
             jax.ShapeDtypeStruct(outer.shape, f32),
             jax.ShapeDtypeStruct(moment.shape, f32),
         ),
         in_specs=[pl.BlockSpec(memory_space=pltpu.SMEM), pl.BlockSpec(memory_space=pltpu.VMEM)]
-        + [any_space] * 7,
+        + [any_space] * 10,
         out_specs=(any_space,) * 6,
         scratch_shapes=[
             pltpu.VMEM(ig.shape, bf16),
             pltpu.VMEM(kv.shape, bf16),
+            *(pltpu.VMEM(term.shape, bf16) for term in terms),
             pltpu.VMEM((rows, cols), f32),
             pltpu.VMEM((rows, cols), bf16),
             pltpu.VMEM((rows, lanes), f32),
@@ -548,18 +562,18 @@
         ],
         compiler_params=pltpu.CompilerParams(vmem_limit_bytes=60 * 1024 * 1024),
         name="finish",
-    )(order, gain, ig, kv, u, drift, weight, outer, moment)
+    )(order, gain, ig, kv, *terms, drift, weight, outer, moment)
 
 
 def on_device(
     tokens, kv_weight, norm_gain, cotangent, global_params, momentum, local_params, fragment_order
 ):
     weight = kv_weight[0]
-    kv, ig, u, drift = layer(
+    kv, ig, *terms, drift = layer(
         tokens, weight, norm_gain, cotangent, global_params, local_params[0], fragment_order
     )
     keys_values, input_grad, weight_grad, gain_grad, new_params, new_momentum = finish(
-        lax.axis_size("replica"), fragment_order, ig, kv, u, drift, weight, norm_gain, global_params, momentum
+        lax.axis_size("replica"), fragment_order, ig, kv, terms, drift, weight, norm_gain, global_params, momentum
     )
     return (keys_values, input_grad, weight_grad[None], gain_grad, new_params, new_momentum)
 

time: 133 us -> 130 us (0.977)
  Pallas kernels: 133 us -> 130 us
    pallas_call x1, Pallas kernels: 122 us -> 118 us  [layer(): pl.pallas_call(functools.partial(layer_kernel, features), out_shape=(jax....]
where the time goes in v3:
time: 130 us
  Pallas kernels  130 us (100%)
    pallas_call x1, Pallas kernels, layer(): pl.pallas_call(functools.partial(layer_kernel, features), out_shape=(jax....  118 us
    pallas_call x1, Pallas kernels, finish(): pl.pallas_call(functools.partial(finish_kernel, replicas), out_shape=(jax...  11.6 us

profile of v3, /device:TPU:0, one launch (start us, length us, event | category | flops | bytes accessed | tf_op | source)
XLA Modules:
  0.0 130.3 jit_solution(11583589671101271753)
XLA Ops:
  0.6 118.0 %layer.1 = (bf16[512,1024]{1,0:T(8,128)(2,1)}, bf16[512,8192]{1,0:T(8,128)(2,1)}, bf16[512,1024]{1,0:T(8,128)(2,1)}, bf16[2,288,1024]{2,1,0:T(8,128)(2,1)}, bf16...) custom-call(s32[4]{0:T(128)} %order.3, bf16[1,512]{1,0:T(2,128)(2,1)} %gain.3, ...), custom_call_target="tpu_custom_call" | custom-call | flops 25769803776 | bytes 419430400 | tf_op jit(solution)/shard_map/layer/pallas_call | solution.py:411
  118.7 11.6 %finish.1 = (bf16[512,1024]{1,0:T(8,128)(2,1)}, bf16[512,8192]{1,0:T(8,128)(2,1)}, f32[512,1024]{1,0:T(8,128)}, f32[1,512]{1,0:T(1,128)}, f32[4,64,1024]{2,1,0:T(8,128)}, /*index=5*/f32[4,64,1024]{2,1,0:T(8,128)}) custom-call(s32[4]{0:T(128)} %order.3, bf16[1,512]{1,0:T(2,128)(2,1)} %gain.3, bf16[512,8192]{1,0:T(8,128)(2,1)} %get-tuple-element.19.ig_in, ...), custom_call_target="tpu_custom_call" | custom-call | tf_op jit(solution)/shard_map/finish/pallas_call | solution.py:536

commit v4 on v3

--- a/solution.py
+++ b/solution.py
@@ -446,7 +446,7 @@
             pltpu.SemaphoreType.DMA((32,)),
         ],
         compiler_params=pltpu.CompilerParams(
-            collective_id=0, has_side_effects=True, vmem_limit_bytes=60 * 1024 * 1024
+            collective_id=0, has_side_effects=True, vmem_limit_bytes=47 * 1024 * 1024
         ),
         cost_estimate=pl.CostEstimate(
             flops=6 * toks * features * cols, bytes_accessed=400 * 1024 * 1024, transcendentals=0
@@ -560,7 +560,7 @@
             pltpu.VMEM(moment.shape, f32),
             pltpu.SemaphoreType.DMA((32,)),
         ],
-        compiler_params=pltpu.CompilerParams(vmem_limit_bytes=60 * 1024 * 1024),
+        compiler_params=pltpu.CompilerParams(vmem_limit_bytes=50 * 1024 * 1024),
         name="finish",
     )(order, gain, ig, kv, *terms, drift, weight, outer, moment)
 

time: 130 us -> 133 us (1.023)
  local copies, waits for them, and re-layouts: 0 us -> 4.74 us
  Pallas kernels: 130 us -> 127 us
    unnamed x0 -> x14, local copies, waits for them, and re-layouts: none -> 4.74 us
    pallas_call x1, Pallas kernels: 11.6 us -> 9.74 us  [finish(): pl.pallas_call(functools.partial(finish_kernel, replicas), out_shape=(jax...]
where the time goes in v4:
time: 133 us
  Pallas kernels  127 us (95%)
  local copies, waits for them, and re-layouts  4.74 us (4%)
    pallas_call x1, Pallas kernels, layer(): pl.pallas_call(functools.partial(layer_kernel, features), out_shape=(jax....  118 us
    pallas_call x1, Pallas kernels, finish(): pl.pallas_call(functools.partial(finish_kernel, replicas), out_shape=(jax...  9.74 us
    unnamed x14, local copies, waits for them, and re-layouts  4.74 us

profile of v4, /device:TPU:0, one launch (start us, length us, event | category | flops | bytes accessed | tf_op | source)
XLA Modules:
  0.0 132.9 jit_solution(18049932914284887945)
XLA Ops:
  0.6 0.0 copy-start
  0.6 1.2 copy-done
  1.9 0.0 copy-start.1
  1.9 0.7 copy-done.1
  2.5 0.0 copy-start.3
  2.5 0.7 copy-done.3
  3.2 0.0 copy-start.5
  3.2 1.2 copy-done.5
  4.4 0.0 copy-start.6
  4.4 0.9 copy-done.6
  5.4 0.0 copy-start.2
  5.4 0.0 copy-start.4
  5.4 117.7 %layer.1 = (bf16[512,1024]{1,0:T(8,128)(2,1)S(1)}, bf16[512,8192]{1,0:T(8,128)(2,1)}, bf16[512,1024]{1,0:T(8,128)(2,1)S(1)}, bf16[2,288,1024]{2,1,0:T(8,128)(2,1...) custom-call(s32[4]{0:T(128)S(1)} %copy-done.3, ...), custom_call_target="tpu_custom_call" | custom-call | flops 25769803776 | bytes 419430400 | tf_op jit(solution)/shard_map/layer/pallas_call | solution.py:411
  123.1 0.0 copy-done.2
  123.1 0.0 copy-done.4
  123.1 9.7 %finish.1 = (bf16[512,1024]{1,0:T(8,128)(2,1)}, bf16[512,8192]{1,0:T(8,128)(2,1)}, f32[512,1024]{1,0:T(8,128)}, f32[1,512]{1,0:T(1,128)}, f32[4,64,1024]{2,1,0:T(8,128)}, /*index=5*/f32[4,64,1024]{2,1,0:T(8,128)}) custom-call(s32[4]{0:T(128)S(1)} %copy-done.4, bf16[1,512]{1,0:T(2,128)(2,1)S(1)} %copy-done.2, bf16[512,8192]{1,0:T(8,128)(2,1)} %get-tuple-element.19.ig_in, ...), custom_call_target="tpu_custom_call" | custom-call | tf_op jit(solution)/shard_map/finish/pallas_call | solution.py:536
Async XLA Ops:
  0.6 1.2 copy-start
  1.9 0.7 copy-start.1
  2.5 0.7 copy-start.3
  3.2 1.2 copy-start.5
  4.4 0.9 copy-start.6
  5.4 117.7 %copy-start.2 = (bf16[1,512]{1,0:T(2,128)(2,1)S(1)}, bf16[1,512]{1,0:T(2,128)(2,1)}, u32[]{:S(2)}) copy-start(bf16[1,512]{1,0:T(2,128)(2,1)} %gain.3) | copy-start | bytes 3076
  5.4 117.7 %copy-start.4 = (s32[4]{0:T(128)S(1)}, s32[4]{0:T(128)}, u32[]{:S(2)}) copy-start(s32[4]{0:T(128)} %order.3) | copy-start | bytes 52
